TPU v7x, 1024 devices: a whole 4x4x32 slice. The times are simulated.
1024 devices in a mesh: row: 16 (over x, z_hi, core), col: 64 (over z_lo, y).
Axes of the slice: x: 4, y: 4, z: 32 (z_hi: 2, z_lo: 16; z = z_hi * 16 + z_lo), core: 2. Of those that a mesh axis runs over, the one named last changes fastest.
Arguments:
- integrals: bfloat16 [2048, 768, 768], P(('row', 'col')), may hold values from -0.875 to 0.875
- block_mask: int32 [2048, 6, 6], P(('row', 'col')), may hold values 0 or 1
- block_sizes: int32 [6], replicated, may hold values from 64 to 128
- density: bfloat16 [768, 768], P('col'), may hold values from -0.21875 to 0.21875
Outputs:
- exchange: float32 [768, 768], P('row', 'col')
All inputs are finite; a program needn't handle non-finite values. No bound on the sum of `block_mask` on one device may be relied on, other than what follows from the above.
Results may differ from a plain program's by a relative error of at most 0.0029.
Values may be sent and summed in bfloat16 or wider, within the bound.
A program may use at most 32 MiB of HBM per device.

v0:
```python
import jax
import jax.numpy as jnp
from jax import lax
from jax.sharding import PartitionSpec as P


def shards(integrals, block_mask, block_sizes, density):
    functions = integrals.shape[1]
    blocks = block_mask.shape[1]
    block_width = functions // blocks
    index = jnp.arange(functions, dtype=jnp.int32)
    member = (index[:, None] // block_width == jnp.arange(blocks, dtype=jnp.int32)[None, :]).astype(
        jnp.int32
    )
    limits = jnp.sum(member * block_sizes[None, :], axis=1)
    present = (index % block_width < limits).astype(jnp.int32)
    expanded = jnp.repeat(jnp.repeat(block_mask, block_width, 1), block_width, 2)
    expanded = expanded * present[None, :, None] * present[None, None, :]
    screened = integrals * expanded.astype(integrals.dtype)
    whole_density = lax.all_gather(density, "col", axis=0, tiled=True)
    contracted = jnp.einsum(
        "pms,sl->pml", screened, whole_density, preferred_element_type=jnp.float32
    ).astype(jnp.bfloat16)
    row_part = lax.psum_scatter(
        jnp.einsum("pml,pnl->mn", contracted, screened, preferred_element_type=jnp.float32),
        "row",
        scatter_dimension=0,
        tiled=True,
    )
    return lax.psum_scatter(row_part, "col", scatter_dimension=1, tiled=True)


def solution(mesh):
    return jax.shard_map(
        shards,
        mesh=mesh,
        in_specs=(
            P(("row", "col"), None, None),
            P(("row", "col"), None, None),
            P(),
            P("col", None),
        ),
        out_specs=P("row", "col"),
        check_vma=False,
    )
```

profile of v0, /device:TPU:24, one launch (start us, length us, event | category | flops | bytes accessed | tf_op | source)
XLA Modules:
  0.0 2299.9 jit_solution(9964259165414362543)
XLA Ops:
  6.5 0.0 all-gather.3.cloned.1.call-start
  6.5 0.7 all-gather.3.cloned.1.call-update
  7.3 0.0 copy-start.1
  7.3 0.0 copy-start.2
  7.3 0.0 reduce-scatter.3.cloned.1.call-start
  7.3 2.8 copy.25
  10.2 0.0 copy-done.1
  10.2 0.1 copy.23
  10.3 0.1 broadcast_in_dim.4
  10.4 0.0 copy-done.2
  10.4 0.1 select_reduce_fusion
  10.5 2.2 fusion.2
  12.7 695.2 %all-gather.3.cloned.1.call-done = bf16[64,12,768]{2,1,0:T(8,128)(2,1)} async-done(((bf16[1,12,768]{2,1,0:T(8,128)(2,1)}), bf16[64,12,768]{2,1,0:T(8,128)(2,1)}) %all-gather.3.cloned.1.call-update) | async-done | bytes 1179664 | tf_op jit(solution)/shard_map/all_gather | solution.py:20
  707.9 2.2 reshape.74
  710.2 0.0 copy-done
  710.2 6.0 fusion.5
  716.2 0.0 reduce-scatter.3.cloned.1.call-update
  716.2 0.0 all-reduce.3.cloned.1.call-start
  716.3 215.1 %reduce-scatter.3.cloned.1.call-done = f32[48,768]{1,0:T(8,128)} async-done(((f32[768,768]{1,0:T(8,128)}), f32[48,768]{1,0:T(8,128)}) %reduce-scatter.3.cloned.1.call-update) | async-done | bytes 147472 | tf_op jit(solution)/shard_map/reduce_scatter | solution.py:24
  931.4 0.0 all-reduce.3.cloned.1.call-update
  931.4 1.3 dynamic-slice
  933.4 1358.5 %all-reduce.3.cloned.1.call-done = f32[48,768]{1,0:T(8,128)} async-done(((f32[48,768]{1,0:T(8,128)}), f32[48,768]{1,0:T(8,128)}) %all-reduce.3.cloned.1.call-update) | async-done | bytes 147472
  2291.8 0.9 constant_dynamic-slice_fusion
  2292.7 0.7 copy.28
  (5 shorter events, 0.0 us)
Async XLA Ops:
  6.5 701.4 %all-gather.3.cloned.1.call-start = ((), (), s32[]{:S(2)}) async-start(), calls=%async_computation.2 | async-start | bytes 1597440 | tf_op jit(solution)/shard_map/all_gather | solution.py:20
  7.3 2.9 copy-start.1
  7.3 3.2 copy-start.2
  7.3 924.1 %reduce-scatter.3.cloned.1.call-start = ((), (), s32[]{:S(2)}) async-start(), calls=%async_computation.1 | async-start | bytes 2506752 | tf_op jit(solution)/shard_map/reduce_scatter | solution.py:24
  12.7 697.5 %copy-start = (bf16[2,768,768]{1,2,0:T(8,128)(2,1)S(1)}, bf16[2,768,768]{1,2,0:T(8,128)(2,1)}, u32[]{:S(2)}) copy-start(bf16[2,768,768]{1,2,0:T(8,128)(2,1)} %fusion.2) | copy-start | bytes 7077892
  716.2 1575.6 %all-reduce.3.cloned.1.call-start = ((), (), s32[]{:S(2)}) async-start(), calls=%async_computation.3 | async-start | bytes 294912
Sparse Core Ops, SparseCore 0:
  10.0 697.8 all-gather.2
  716.3 215.0 reduce-scatter.2
  934.9 1356.8 all-reduce.2
where the time goes:
time: 2320 us; the launch traced here: 2300 us
  waiting for transfers between devices  2270 us (98%)
    unnamed x4, waiting for transfers between devices  1360 us
    all_gather x1, waiting for transfers between devices, shards(): whole_density = lax.all_gather(density, 'col', axis=0, tiled=True)  695 us
    reduce_scatter x1, waiting for transfers between devices, shards(): lax.psum_scatter(jnp.einsum('pml,pnl->mn', contracted, screened, preferre...  215 us
  transfers between devices with their start and end apart: 3, of which 3 were waited for; matrix products, arithmetic and copies ran while one was open for 0% of the time, Pallas kernels for 0%

commit v1 on v0

v1 whole, which is shorter than its diff:
```python
import jax
import jax.numpy as jnp
from jax import lax
from jax.experimental import pallas as pl
from jax.experimental.pallas import tpu as pltpu
from jax.sharding import PartitionSpec as P

MESH = pl.DeviceIdType.MESH
F32 = jnp.float32
BF16 = jnp.bfloat16

Z_GATHER = [d for d in range(-8, 8) if d != 0]
PLANE = [(dx, dy) for dx in range(4) for dy in range(4) if (dx, dy) != (0, 0)]
Z_NEAR = [-2, -1, 1]
Z_FAR = [-12, -8, -4, 4, 8, 12, 16]
Z_GREET = [d for d in range(-8, 9) if d != 0] + [-12, 12, 16]


def device(x, y, z, core):
    return ((x * 2 + z // 16) * 2 + core, (z % 16) * 4 + y)


def wrap(value, size):
    return lax.rem(value + size, size)


def iota(shape, dim):
    return lax.broadcasted_iota(jnp.int32, shape, dim)


def dot(a, b):
    return jnp.dot(a, b, preferred_element_type=F32)


def dot_nt(a, b):
    return lax.dot_general(a, b, (((1,), (1,)), ((), ())), preferred_element_type=F32)


def kernel(
    mask_ref, sizes_ref, integrals_ref, density_ref, out_ref,
    raw, screened, left, right, swap, spread, squeeze, tile, dens, contracted,
    k_send, k_land, p_send, p_land, by_column, n_land, f_send, f_land,
    load_sem, zs, zr, ps, pr, cs, cr, ks, kr, qs, qr, ns, nr, fs, fr,
):
    row, col = lax.axis_index("row"), lax.axis_index("col")
    x, y = row // 4, col % 4
    z, core = (row // 2) % 2 * 16 + col // 4, row % 2
    z_lo = col // 4
    sibling = device(x, y, z, 1 - core)

    def at_z(d):
        return device(x, y, wrap(z + d, 32), core)

    def in_plane(dx, dy):
        return device((x + dx) % 4, (y + dy) % 4, z, core)

    def remote(src, dst, send, recv, target):
        return pltpu.make_async_remote_copy(
            src_ref=src, dst_ref=dst, send_sem=send, recv_sem=recv,
            device_id=target, device_id_type=MESH,
        )

    barrier = pltpu.get_barrier_semaphore()
    greet = [at_z(d) for d in Z_GREET] + [in_plane(*d) for d in PLANE] + [sibling]
    for target in greet:
        pl.semaphore_signal(barrier, inc=1, device_id=target, device_id_type=MESH)

    load = pltpu.make_async_copy(integrals_ref, raw, load_sem)
    load.start()

    slot = z_lo % 4 * 4 + z_lo // 4
    column = pl.multiple_of(core * 384 + lax.rem(x, 3) * 128, 128)
    pad = (iota((16, 12), 0) == iota((16, 12), 1)).astype(BF16)
    tile[slot] = dot(pad, density_ref[:, pl.ds(column, 128)]).astype(BF16)

    r, c = iota((192, 256), 0), iota((192, 256), 1)
    squeeze[...] = ((r // 12) * 16 + r % 12 == c).astype(BF16)

    @pl.loop(0, 6)
    def _(i):
        start = pl.multiple_of(i * 128, 128)
        r, c = iota((128, 768), 0) + start, iota((128, 768), 1)
        moved = r % 192 // 12 % 4 * 192 + r % 192 // 48 * 48 + r // 192 * 12 + r % 12
        swap[pl.ds(start, 128)] = (moved == c).astype(BF16)
        tail = r - 512
        part = jnp.where(r < 512, r // 128, tail // 64)
        q = jnp.where(r < 512, r % 128, tail % 64 + 128)
        source = q % 48 // 12 * 192 + q // 48 * 48 + part * 12 + q % 12
        spread[pl.ds(start, 128)] = (source == c).astype(BF16)

    load.wait()

    lane = iota((1, 128), 1)
    for i in range(6):
        present_row = (iota((128, 128), 0) < sizes_ref[i]).astype(F32).astype(BF16)
        for p in range(2):
            for k in range(6):
                keep = (lane < sizes_ref[k] * mask_ref[p, i, k]).astype(F32).astype(BF16)
                block = raw[p, pl.ds(i * 128, 128), pl.ds(k * 128, 128)]
                screened[p, pl.ds(i * 128, 128), pl.ds(k * 128, 128)] = block * (present_row * keep)

    pl.semaphore_wait(barrier, len(greet))

    z_copies = [
        remote(tile.at[slot], tile.at[slot], zs.at[n], zr.at[n], at_z(d))
        for n, d in enumerate(Z_GATHER)
    ]

    @pl.when(x < 3)
    def _():
        for copy in z_copies:
            copy.start()

    @pl.loop(0, 8)
    def _(i):
        p, part = i // 4, i % 4
        rows = pl.ds(pl.multiple_of(part * 192, 192), 192)
        moved = dot(screened[p, rows], swap[...]).astype(BF16)
        for zh in range(2):
            for other in range(2):
                half = (other + core + 1) % 2
                to = pl.multiple_of(half * 384 + part * 96 + zh * 48, 16)
                at = zh * 96 + other * 48
                left[p, pl.ds(to, 48)] = moved[at : at + 48]
        right[p, rows] = dot(spread[rows], screened[p]).astype(BF16)

    @pl.when(x < 3)
    def _():
        for copy in z_copies:
            copy.wait()
        mine = pl.ds(pl.multiple_of(y * 192, 16), 192)
        dens[core, x, mine] = dot(squeeze[...], tile[...].reshape(256, 128)).astype(BF16)
        for n, (dx, dy) in enumerate(PLANE):
            remote(
                dens.at[core, x, mine], dens.at[core, x, mine], ps.at[n], pr.at[x * 4 + y],
                in_plane(dx, dy),
            ).start()

    for sx in range(3):
        for sy in range(4):
            n = sx * 4 + sy
            block = dens.at[core, sx, pl.ds(sy * 192, 192)]

            @pl.when(jnp.logical_or(x != sx, y != sy))
            def _():
                remote(block, block, ps.at[0], pr.at[n], sibling).wait_recv()

            remote(block, block, cs.at[n], cr.at[n], sibling).start()

    def contract(half):
        density = jnp.concatenate([dens[half, t] for t in range(3)], axis=1)

        @pl.loop(0, 4)
        def _(i):
            p, rows = i // 2, pl.ds(pl.multiple_of(i % 2 * 384, 384), 384)
            contracted[p, half, rows] = dot(left[p, rows], density).astype(BF16)

    contract(core)
    for sx in range(3):
        for sy in range(4):
            n = sx * 4 + sy
            block = dens.at[1 - core, sx, pl.ds(sy * 192, 192)]
            remote(block, block, cs.at[n], cr.at[n], sibling).wait_recv()
    contract(1 - core)

    def exchange(half, chunk):
        total = None
        for p in range(2):
            rows = pl.ds(half * 384, 384)
            a = jnp.concatenate([contracted[p, 0, rows], contracted[p, 1, rows]], axis=1)
            term = dot_nt(a, right[p, pl.ds(chunk * 256, 256)])
            total = term if total is None else total + term
        return total

    k_copies = [
        remote(k_send.at[n], k_land.at[n], ks.at[n], kr.at[n], sibling) for n in range(3)
    ]
    for n in range(3):
        k_send[n] = exchange(0, n).astype(BF16)
        k_copies[n].start()
    low = iota((48, 128), 1) < 64
    for n in range(3):
        own = exchange(1, n)
        k_copies[n].wait_recv()
        total = own + k_land[n].astype(F32)
        for tx in range(4):
            for half in range(2):
                block = total[tx * 96 : tx * 96 + 96, half * 128 : half * 128 + 128]
                if n < 2:
                    p_send[tx * 4 + n * 2 + half, :96] = block.astype(BF16)
                else:
                    first, second = block[:48], block[48:]
                    even = jnp.where(low, first, pltpu.roll(second, 64, 1))
                    odd = jnp.where(low, pltpu.roll(first, 64, 1), second)
                    p_send[tx * 4 + half * 2, 96:] = even.astype(BF16)
                    p_send[tx * 4 + half * 2 + 1, 96:] = odd.astype(BF16)

    q_copies = []
    for n, (dx, dy) in enumerate(PLANE):
        target = (x + dx) % 4 * 4 + (y + dy) % 4
        q_copies.append(
            remote(p_send.at[target], p_land.at[n], qs.at[n], qr.at[n], in_plane(dx, dy))
        )
        q_copies[-1].start()
    total = p_send[x * 4 + y].astype(F32)
    for n, copy in enumerate(q_copies):
        copy.wait_recv()
        total = total + p_land[n].astype(F32)

    zeros = jnp.zeros((80, 128), F32)
    by_column[:128] = jnp.transpose(jnp.concatenate([total[:96], zeros[:32]], axis=0))
    turned = jnp.transpose(jnp.concatenate([total[96:], zeros], axis=0))
    lanes = iota((64, 128), 1)
    by_column[128:] = jnp.where(lanes < 48, turned[:64], pltpu.roll(turned[64:], 48, 1))

    n_copies = []
    for n, d in enumerate(Z_NEAR):
        at = pl.multiple_of((z + d + 32) % 4 * 48, 16)
        n_copies.append(
            remote(by_column.at[pl.ds(at, 48)], n_land.at[n], ns.at[n], nr.at[n], at_z(d))
        )
        n_copies[-1].start()
    total = by_column[pl.ds(pl.multiple_of(z % 4 * 48, 16), 48)]
    for n, copy in enumerate(n_copies):
        copy.wait_recv()
        total = total + n_land[n]

    lanes = iota((8, 128), 1)
    for b in range(4):
        first = total[b * 12 : b * 12 + 8]
        second = jnp.concatenate([total[b * 12 + 8 : b * 12 + 12]] * 2, axis=0)
        f_send[b] = jnp.where(lanes < 48, first, pltpu.roll(second, 48, 1))
        f_send[4 + b] = jnp.where(lanes < 48, pltpu.roll(first, 80, 1), second)
    f_copies = []
    for n, d in enumerate(Z_FAR):
        target = wrap(z + d, 32) // 4
        f_copies.append(
            remote(f_send.at[target], f_land.at[n], fs.at[n], fr.at[n], at_z(d))
        )
        f_copies[-1].start()
    total = f_send[z // 4]
    for n, copy in enumerate(f_copies):
        copy.wait_recv()
        total = total + f_land[n]
    turned = jnp.transpose(jnp.concatenate([total, jnp.zeros((120, 128), F32)], axis=0))
    out_ref[:, :8] = turned[:48, :8]
    out_ref[:, 8:] = turned[48:96, :4]

    @pl.when(x < 3)
    def _():
        mine = pl.ds(pl.multiple_of(y * 192, 16), 192)
        for n, (dx, dy) in enumerate(PLANE):
            remote(
                dens.at[core, x, mine], dens.at[core, x, mine], ps.at[n], pr.at[x * 4 + y],
                in_plane(dx, dy),
            ).wait_send()

    for n in range(12):
        block = dens.at[core, n // 4, pl.ds(n % 4 * 192, 192)]
        remote(block, block, cs.at[n], cr.at[n], sibling).wait_send()
    for copy in k_copies + q_copies + n_copies + f_copies:
        copy.wait_send()


def shards(integrals, block_mask, block_sizes, density):
    dma = lambda n: pltpu.SemaphoreType.DMA((n,))
    vmem = lambda *shape: pltpu.VMEM(shape, BF16)
    return pl.pallas_call(
        kernel,
        out_shape=jax.ShapeDtypeStruct((48, 12), F32),
        in_specs=[
            pl.BlockSpec(memory_space=pltpu.SMEM),
            pl.BlockSpec(memory_space=pltpu.SMEM),
            pl.BlockSpec(memory_space=pl.ANY),
            pl.BlockSpec(memory_space=pltpu.VMEM),
        ],
        out_specs=pl.BlockSpec(memory_space=pltpu.VMEM),
        scratch_shapes=[
            vmem(2, 768, 768),
            vmem(2, 768, 768),
            vmem(2, 768, 768),
            vmem(2, 768, 768),
            vmem(768, 768),
            vmem(768, 768),
            vmem(192, 256),
            vmem(16, 16, 128),
            vmem(2, 3, 768, 128),
            vmem(2, 2, 768, 384),
            vmem(3, 384, 256),
            vmem(3, 384, 256),
            vmem(16, 144, 128),
            vmem(15, 144, 128),
            pltpu.VMEM((192, 128), F32),
            pltpu.VMEM((3, 48, 128), F32),
            pltpu.VMEM((8, 8, 128), F32),
            pltpu.VMEM((7, 8, 128), F32),
            pltpu.SemaphoreType.DMA,
            dma(15), dma(15),
            dma(15), dma(12),
            dma(12), dma(12),
            dma(3), dma(3),
            dma(15), dma(15),
            dma(3), dma(3),
            dma(7), dma(7),
        ],
        compiler_params=pltpu.CompilerParams(
            collective_id=0, has_side_effects=True, vmem_limit_bytes=48 * 1024 * 1024
        ),
        name="exchange",
    )(block_mask, block_sizes, integrals, density)


def solution(mesh):
    return jax.shard_map(
        shards,
        mesh=mesh,
        in_specs=(
            P(("row", "col"), None, None),
            P(("row", "col"), None, None),
            P(),
            P("col", None),
        ),
        out_specs=P("row", "col"),
        check_vma=False,
    )
```

time: 2320 us -> 86.3 us (0.04)
  waiting for transfers between devices: 2270 us -> 0 us
  Pallas kernels: 0 us -> 81.5 us
    unnamed x4 -> x0, waiting for transfers between devices: 1360 us -> none
    all_gather x1 -> x0, waiting for transfers between devices: 695 us -> none  [shards(): whole_density = lax.all_gather(density, 'col', axis=0, tiled=True)]
    reduce_scatter x1 -> x0, waiting for transfers between devices: 215 us -> none  [shards(): lax.psum_scatter(jnp.einsum('pml,pnl->mn', contracted, screened, preferre...]
    pallas_call x0 -> x1, Pallas kernels: none -> 81.5 us  [shards(): pl.pallas_call(kernel, out_shape=jax.ShapeDtypeStruct((48, 12), F32), in_...]
  transfers between devices with their start and end apart: 3 -> 0, of which waited for: 3 -> 0; matrix products, arithmetic and copies ran while one was open for 0% -> 0% of each run, Pallas kernels for 0% -> 0%
where the time goes in v1:
time: 86.3 us; the launch traced here: 86 us
  Pallas kernels  81.5 us (94%)
  local copies, waits for them, and re-layouts  4.42 us (5%)
    pallas_call x1, Pallas kernels, shards(): pl.pallas_call(kernel, out_shape=jax.ShapeDtypeStruct((48, 12), F32), in_...  81.5 us
    unnamed x7, local copies, waits for them, and re-layouts  3.75 us

profile of v1, /device:TPU:24, one launch (start us, length us, event | category | flops | bytes accessed | tf_op | source)
XLA Modules:
  0.0 86.0 jit_solution(16244554759056147142)
XLA Ops:
  0.0 0.7 copy.5.mask_ref
  0.7 0.0 copy-start
  0.7 1.7 %copy-done = bf16[2,768,768]{2,1,0:T(8,128)(2,1)S(1)} copy-done((bf16[2,768,768]{2,1,0:T(8,128)(2,1)S(1)}, bf16[2,768,768]{2,1,0:T(8,128)(2,1)}, u32[]{:S(2)}) %copy-start) | copy-done | bytes 2359320
  2.4 0.0 copy-start.1
  2.4 0.7 copy-done.1
  3.1 0.0 copy-start.2
  3.1 0.7 copy-done.2
  3.8 81.5 %exchange.1 = f32[48,12]{1,0:T(8,128)S(1)} custom-call(s32[2,6,6]{2,1,0:T(8,128)S(1)} %copy.5.mask_ref, s32[6]{0:T(128)S(1)} %copy-done.2, bf16[2,768,768]{2,1,0:T(8,128)(2,1)S(1)} %copy-done, bf16[12,768]{1,0:T(8,128)(2,1)S(1)} %copy-done.1), custom_call_target="tpu_custom_call" | custom-call | tf_op jit(solution)/shard_map/exchange/pallas_call | solution.py:268
  85.3 0.7 copy.6
Async XLA Ops:
  0.7 1.7 %copy-start = (bf16[2,768,768]{2,1,0:T(8,128)(2,1)S(1)}, bf16[2,768,768]{2,1,0:T(8,128)(2,1)}, u32[]{:S(2)}) copy-start(bf16[2,768,768]{2,1,0:T(8,128)(2,1)} %integrals_ref.1) | copy-start | bytes 7077892
  2.4 0.7 copy-start.1
  3.1 0.7 copy-start.2

commit v2 on v1

v2 whole, which is shorter than its diff:
```python
import jax
import jax.numpy as jnp
from jax import lax
from jax.experimental import pallas as pl
from jax.experimental.pallas import tpu as pltpu
from jax.sharding import PartitionSpec as P

MESH = pl.DeviceIdType.MESH
F32 = jnp.float32
BF16 = jnp.bfloat16

Z_SLOTS = [n - 4 if n < 12 else n - 20 for n in range(16)]
Z_OWN = Z_SLOTS.index(0)
PLANE = [(dx, dy) for dx in range(4) for dy in range(4) if (dx, dy) != (0, 0)]
Z_NEAR = [-2, -1, 1]
Z_FAR = [-12, -8, -4, 4, 8, 12, 16]
Z_GREET = sorted((d for d in range(-8, 9) if d != 0), key=lambda d: -abs(d))


def device(x, y, z, core):
    return ((x * 2 + z // 16) * 2 + core, (z % 16) * 4 + y)


def wrap(value, size):
    return lax.rem(value + size, size)


def iota(shape, dim):
    return lax.broadcasted_iota(jnp.int32, shape, dim)


def dot(a, b):
    return jnp.dot(a, b, preferred_element_type=F32)


def dot_nt(a, b):
    return lax.dot_general(a, b, (((1,), (1,)), ((), ())), preferred_element_type=F32)


def kernel(
    mask_hbm, sizes_hbm, integrals_ref, density_hbm, out_ref,
    mask_ref, sizes_ref, density_ref,
    raw, screened, left, right, swap, spread, squeeze, tile, own3, tile3, dens, contracted,
    k_send, k_land, p_send, p_land, by_column, n_land, f_send, f_land,
    load_sem, ready, zs, zr, ps, pr, cs, cr, ks, kr, qs, qr, ns, nr, fs, fr,
):
    row, col = lax.axis_index("row"), lax.axis_index("col")
    x, y = row // 4, col % 4
    z, core = (row // 2) % 2 * 16 + col // 4, row % 2
    z_lo = col // 4
    sibling = device(x, y, z, 1 - core)

    def at_z(d):
        return device(x, y, wrap(z + d, 32), core)

    def in_plane(dx, dy):
        return device((x + dx) % 4, (y + dy) % 4, z, core)

    def remote(src, dst, send, recv, target):
        return pltpu.make_async_remote_copy(
            src_ref=src, dst_ref=dst, send_sem=send, recv_sem=recv,
            device_id=target, device_id_type=MESH,
        )

    barrier = pltpu.get_barrier_semaphore()
    greet = [at_z(d) for d in Z_GREET] + [in_plane(*d) for d in PLANE] + [sibling]
    for target in greet:
        pl.semaphore_signal(barrier, inc=1, device_id=target, device_id_type=MESH)

    loads = [
        pltpu.make_async_copy(density_hbm, density_ref, load_sem.at[0]),
        pltpu.make_async_copy(sizes_hbm, sizes_ref, load_sem.at[1]),
        pltpu.make_async_copy(mask_hbm, mask_ref, load_sem.at[2]),
        pltpu.make_async_copy(integrals_ref, raw, load_sem.at[3]),
    ]
    for load in loads:
        load.start()

    r, c = iota((96, 128), 0), iota((96, 128), 1)
    squeeze[...] = ((r // 12) * 16 + r % 12 == c).astype(BF16)

    loads[0].wait()
    pad = (iota((16, 12), 0) == iota((16, 12), 1)).astype(BF16)
    for t in range(3):
        column = pl.multiple_of(core * 384 + t * 128, 128)
        own3[t] = dot(pad, density_ref[:, pl.ds(column, 128)]).astype(BF16)
    tile[Z_OWN] = own3[lax.rem(x, 3)]

    for load in loads[1:]:
        load.wait()

    lane = iota((1, 128), 1)
    for i in range(6):
        present_row = (iota((128, 128), 0) < sizes_ref[i]).astype(F32).astype(BF16)
        for p in range(2):
            for k in range(6):
                keep = (lane < sizes_ref[k] * mask_ref[i, p, k]).astype(F32).astype(BF16)
                block = raw[p, pl.ds(i * 128, 128), pl.ds(k * 128, 128)]
                screened[p, pl.ds(i * 128, 128), pl.ds(k * 128, 128)] = block * (present_row * keep)

    pl.semaphore_wait(barrier, len(greet))
    for d in (-8, 8):
        pl.semaphore_signal(ready, inc=1, device_id=at_z(d), device_id_type=MESH)

    def z_copy(n):
        if n < 12:
            return remote(tile.at[Z_OWN], tile.at[n], zs.at[n], zr.at[n], at_z(Z_SLOTS[n]))
        return remote(own3, tile3.at[n - 12], zs.at[n], zr.at[n], at_z(Z_SLOTS[n]))

    @pl.when(x < 3)
    def _():
        for n in sorted(range(12), key=lambda n: -abs(Z_SLOTS[n])):
            if n != Z_OWN:
                z_copy(n).start()

    @pl.when(x == 3)
    def _():
        for n in range(12, 16):
            z_copy(n).start()

    @pl.loop(0, 6)
    def _(i):
        start = pl.multiple_of(i * 128, 128)
        r, c = iota((128, 768), 0) + start, iota((128, 768), 1)
        origin = (z_lo + 36 - c // 384 * 8 - c % 96 // 12) % 16
        swap[pl.ds(start, 128)] = (origin * 48 + c % 384 // 96 * 12 + c % 12 == r).astype(BF16)
        tail = r - 512
        part = jnp.where(r < 512, r // 128, tail // 64)
        q = jnp.where(r < 512, r % 128, tail % 64 + 128)
        source = q % 48 // 12 * 192 + q // 48 * 48 + part * 12 + q % 12
        spread[pl.ds(start, 128)] = (source == c).astype(BF16)

    def prepare(p):
        @pl.loop(0, 4)
        def _(part):
            rows = pl.ds(pl.multiple_of(part * 192, 192), 192)
            moved = dot(screened[p, rows], swap[...]).astype(BF16)
            for zh in range(2):
                for other in range(2):
                    half = (other + core + 1) % 2
                    to = pl.multiple_of(half * 384 + part * 96 + zh * 48, 16)
                    at = zh * 96 + other * 48
                    left[p, pl.ds(to, 48)] = moved[at : at + 48]
            right[p, rows] = dot(spread[rows], screened[p]).astype(BF16)

    prepare(0)

    def block(g, sx, sy):
        at = pl.multiple_of(g * 384 + sy * 96, 16)
        return dens.at[core, sx, pl.ds(at, 96 if g == 0 else 48)]

    def block3(sy):
        return dens.at[core, :, pl.ds(pl.multiple_of(384 + sy * 96 + 48, 16), 48)]

    def plane_copy(g, n):
        mine = block(g, x, y)
        return remote(mine, mine, ps.at[g, n], pr.at[g * 12 + x * 4 + y], in_plane(*PLANE[n]))

    def plane_copy3(n):
        mine = block3(y)
        return remote(mine, mine, ps.at[1, n], pr.at[24 + y], in_plane(*PLANE[n]))

    @pl.when(x < 3)
    def _():
        for g in range(2):
            slots = range(8) if g == 0 else range(8, 12)
            for n in slots:
                if n != Z_OWN:
                    z_copy(n).wait()
            size = len(slots)
            rows = tile[slots[0] : slots[0] + size].reshape(size * 16, 128)
            packed = dot(squeeze[: size * 12, : size * 16], rows).astype(BF16)
            dens[core, x, pl.ds(pl.multiple_of(g * 384 + y * 96, 16), size * 12)] = packed
            for n in range(len(PLANE)):
                plane_copy(g, n).start()

    @pl.when(x == 3)
    def _():
        for n in range(12, 16):
            z_copy(n).wait()
        for t in range(3):
            packed = dot(squeeze[:48, :64], tile3[:, t].reshape(64, 128)).astype(BF16)
            dens[core, t, pl.ds(pl.multiple_of(384 + y * 96 + 48, 16), 48)] = packed
        for n in range(len(PLANE)):
            plane_copy3(n).start()

    prepare(1)

    c_copies = []
    for g in range(2):
        if g == 1:
            for sy in range(4):

                @pl.when(jnp.logical_or(x != 3, y != sy))
                def _():
                    remote(block3(sy), block3(sy), ps.at[0, 0], pr.at[24 + sy], sibling).wait_recv()

        for sx in range(3):
            for sy in range(4):

                @pl.when(jnp.logical_or(x != sx, y != sy))
                def _():
                    arrived = block(g, sx, sy)
                    remote(
                        arrived, arrived, ps.at[0, 0], pr.at[g * 12 + sx * 4 + sy], sibling
                    ).wait_recv()

            whole = dens.at[core, sx, pl.ds(g * 384, 384)]
            c_copies.append(remote(whole, whole, cs.at[g * 3 + sx], cr.at[g * 3 + sx], sibling))
            c_copies[-1].start()

    def contract(half):
        density = jnp.concatenate([dens[half, t] for t in range(3)], axis=1)

        @pl.loop(0, 4)
        def _(i):
            p, rows = i // 2, pl.ds(pl.multiple_of(i % 2 * 384, 384), 384)
            contracted[p, half, rows] = dot(left[p, rows], density).astype(BF16)

    contract(core)
    for g in range(2):
        for sx in range(3):
            whole = dens.at[1 - core, sx, pl.ds(g * 384, 384)]
            remote(
                whole, whole, cs.at[g * 3 + sx], cr.at[g * 3 + sx], sibling
            ).wait_recv()
    contract(1 - core)

    def exchange(half, chunk):
        total = None
        for p in range(2):
            rows = pl.ds(half * 384, 384)
            a = jnp.concatenate([contracted[p, 0, rows], contracted[p, 1, rows]], axis=1)
            term = dot_nt(a, right[p, pl.ds(chunk * 256, 256)])
            total = term if total is None else total + term
        return total

    k_copies = [
        remote(k_send.at[n], k_land.at[n], ks.at[n], kr.at[n], sibling) for n in range(3)
    ]
    low = iota((48, 128), 1) < 64

    def send_half(n):
        k_send[n] = exchange(0, n).astype(BF16)
        k_copies[n].start()

    def own_half(n):
        own = exchange(1, n)
        k_copies[n].wait_recv()
        total = own + k_land[n].astype(F32)
        for tx in range(4):
            for half in range(2):
                block = total[tx * 96 : tx * 96 + 96, half * 128 : half * 128 + 128]
                if n < 2:
                    p_send[tx * 4 + n * 2 + half, :96] = block.astype(BF16)
                else:
                    first, second = block[:48], block[48:]
                    even = jnp.where(low, first, pltpu.roll(second, 64, 1))
                    odd = jnp.where(low, pltpu.roll(first, 64, 1), second)
                    p_send[tx * 4 + half * 2, 96:] = even.astype(BF16)
                    p_send[tx * 4 + half * 2 + 1, 96:] = odd.astype(BF16)

    parts = [pl.ds(0, 96), pl.ds(96, 48)]

    def send_plane(part, ty):
        for tx in range(4):

            @pl.when(jnp.logical_or(tx != x, ty != y))
            def _():
                slot = (tx - x + 4) % 4 * 4 + (ty - y + 4) % 4
                remote(
                    p_send.at[tx * 4 + ty, parts[part]], p_land.at[slot, parts[part]],
                    qs.at[part, slot], qr.at[part, slot], device(tx, ty, z, core),
                ).start()

    send_half(0)
    send_half(1)
    own_half(0)
    send_plane(0, 0)
    send_plane(0, 1)
    send_half(2)
    own_half(1)
    send_plane(0, 2)
    send_plane(0, 3)
    own_half(2)
    for ty in range(4):
        send_plane(1, ty)

    q_copies = [
        remote(
            p_send.at[0, rows], p_land.at[slot, rows], qs.at[part, slot], qr.at[part, slot], sibling
        )
        for part, rows in enumerate(parts)
        for slot in range(1, 16)
    ]
    sums = []
    for part, rows in enumerate(parts):
        total = p_send[x * 4 + y, rows].astype(F32)
        for slot in range(1, 16):
            q_copies[part * 15 + slot - 1].wait_recv()
            total = total + p_land[slot, rows].astype(F32)
        sums.append(total)

    zeros = jnp.zeros((80, 128), F32)
    by_column[:128] = jnp.transpose(jnp.concatenate([sums[0], zeros[:32]], axis=0))
    turned = jnp.transpose(jnp.concatenate([sums[1], zeros], axis=0))
    lanes = iota((64, 128), 1)
    by_column[128:] = jnp.where(lanes < 48, turned[:64], pltpu.roll(turned[64:], 48, 1))

    n_copies = []
    for n, d in enumerate(Z_NEAR):
        at = pl.multiple_of((z + d + 32) % 4 * 48, 16)
        n_copies.append(
            remote(by_column.at[pl.ds(at, 48)], n_land.at[n], ns.at[n], nr.at[n], at_z(d))
        )
        n_copies[-1].start()
    total = by_column[pl.ds(pl.multiple_of(z % 4 * 48, 16), 48)]
    for n, copy in enumerate(n_copies):
        copy.wait_recv()
        total = total + n_land[n]

    lanes = iota((8, 128), 1)
    for b in range(4):
        first = total[b * 12 : b * 12 + 8]
        second = jnp.concatenate([total[b * 12 + 8 : b * 12 + 12]] * 2, axis=0)
        f_send[b] = jnp.where(lanes < 48, first, pltpu.roll(second, 48, 1))
        f_send[4 + b] = jnp.where(lanes < 48, pltpu.roll(first, 80, 1), second)
    pl.semaphore_wait(ready, 2)
    f_copies = []
    for n, d in enumerate(Z_FAR):
        target = wrap(z + d, 32) // 4
        f_copies.append(
            remote(f_send.at[target], f_land.at[n], fs.at[n], fr.at[n], at_z(d))
        )
        f_copies[-1].start()
    total = f_send[z // 4]
    for n, copy in enumerate(f_copies):
        copy.wait_recv()
        total = total + f_land[n]
    out_ref[:8] = total[:, :48]
    out_ref[8:] = pltpu.roll(total, 80, 1)[:4, :48]

    @pl.when(x < 3)
    def _():
        for g in range(2):
            for n in range(len(PLANE)):
                plane_copy(g, n).wait_send()

    @pl.when(x == 3)
    def _():
        for n in range(len(PLANE)):
            plane_copy3(n).wait_send()

    for copy in c_copies + k_copies + q_copies + n_copies + f_copies:
        copy.wait_send()


def shards(integrals, block_mask, block_sizes, density):
    dma = lambda *shape: pltpu.SemaphoreType.DMA(shape)
    vmem = lambda *shape: pltpu.VMEM(shape, BF16)
    exchange = pl.pallas_call(
        kernel,
        out_shape=pltpu.VMEM((12, 48), F32),
        in_specs=[pl.BlockSpec(memory_space=pltpu.HBM)] * 4,
        out_specs=pl.BlockSpec(memory_space=pltpu.VMEM),
        scratch_shapes=[
            pltpu.SMEM((6, 2, 6), jnp.int32),
            pltpu.SMEM((6,), jnp.int32),
            vmem(12, 768),
            vmem(2, 768, 768),
            vmem(2, 768, 768),
            vmem(2, 768, 768),
            vmem(2, 768, 768),
            vmem(768, 768),
            vmem(768, 768),
            vmem(96, 128),
            vmem(12, 16, 128),
            vmem(3, 16, 128),
            vmem(4, 3, 16, 128),
            vmem(2, 3, 768, 128),
            vmem(2, 2, 768, 384),
            vmem(3, 384, 256),
            vmem(3, 384, 256),
            vmem(16, 144, 128),
            vmem(16, 144, 128),
            pltpu.VMEM((192, 128), F32),
            pltpu.VMEM((3, 48, 128), F32),
            pltpu.VMEM((8, 8, 128), F32),
            pltpu.VMEM((7, 8, 128), F32),
            dma(4),
            pltpu.SemaphoreType.REGULAR,
            dma(16), dma(16),
            dma(2, 15), dma(28),
            dma(6), dma(6),
            dma(3), dma(3),
            dma(2, 16), dma(2, 16),
            dma(3), dma(3),
            dma(7), dma(7),
        ],
        compiler_params=pltpu.CompilerParams(
            collective_id=0, has_side_effects=True, vmem_limit_bytes=60 * 1024 * 1024
        ),
        name="exchange",
    )(jnp.transpose(block_mask, (1, 0, 2)), block_sizes, integrals, density)
    return jnp.transpose(exchange)


def solution(mesh):
    return jax.shard_map(
        shards,
        mesh=mesh,
        in_specs=(
            P(("row", "col"), None, None),
            P(("row", "col"), None, None),
            P(),
            P("col", None),
        ),
        out_specs=P("row", "col"),
        check_vma=False,
    )
```

time: 86.3 us -> 75.3 us (0.87)
  Pallas kernels: 81.5 us -> 74.5 us
  local copies, waits for them, and re-layouts: 4.42 us -> 0.6 us
    pallas_call x1, Pallas kernels: 81.5 us -> 74.5 us  [shards(): pl.pallas_call(kernel, out_shape=pltpu.VMEM((12, 48), F32), in_specs=[pl....]
    unnamed x7 -> x1, local copies, waits for them, and re-layouts: 3.75 us -> 0.6 us
where the time goes in v2:
time: 75.3 us; the launch traced here: 75.1 us
  Pallas kernels  74.5 us (99%)
    pallas_call x1, Pallas kernels, shards(): pl.pallas_call(kernel, out_shape=pltpu.VMEM((12, 48), F32), in_specs=[pl....  74.5 us

profile of v2, /device:TPU:24, one launch (start us, length us, event | category | flops | bytes accessed | tf_op | source)
XLA Modules:
  0.0 75.1 jit_solution(4876834485367222435)
XLA Ops:
  0.0 74.5 %exchange.1 = f32[12,48]{1,0:T(8,128)S(1)} custom-call(s32[6,2,6]{2,1,0:T(2,128)} %bitcast.3, s32[6]{0:T(128)} %sizes_hbm.1, bf16[2,768,768]{2,1,0:T(8,128)(2,1)} %integrals_ref.1, bf16[12,768]{1,0:T(8,128)(2,1)} %density_hbm.1), custom_call_target="tpu_custom_call" | custom-call | tf_op jit(solution)/shard_map/exchange/pallas_call | solution.py:361
  74.5 0.6 copy.6

commit v3 on v2

--- a/solution.py
+++ b/solution.py
@@ -9,12 +9,11 @@
 F32 = jnp.float32
 BF16 = jnp.bfloat16
 
-Z_SLOTS = [n - 4 if n < 12 else n - 20 for n in range(16)]
-Z_OWN = Z_SLOTS.index(0)
+Z_OWN = 4
 PLANE = [(dx, dy) for dx in range(4) for dy in range(4) if (dx, dy) != (0, 0)]
 Z_NEAR = [-2, -1, 1]
 Z_FAR = [-12, -8, -4, 4, 8, 12, 16]
-Z_GREET = sorted((d for d in range(-8, 9) if d != 0), key=lambda d: -abs(d))
+Z_GREET = [-4, 4, -3, 3, -2, 2, -1, 1]
 
 
 def device(x, y, z, core):
@@ -40,9 +39,9 @@
 def kernel(
     mask_hbm, sizes_hbm, integrals_ref, density_hbm, out_ref,
     mask_ref, sizes_ref, density_ref,
-    raw, screened, left, right, swap, spread, squeeze, tile, own3, tile3, dens, contracted,
+    raw, screened, left, right, swap, spread, squeeze, tile, dens, contracted,
     k_send, k_land, p_send, p_land, by_column, n_land, f_send, f_land,
-    load_sem, ready, zs, zr, ps, pr, cs, cr, ks, kr, qs, qr, ns, nr, fs, fr,
+    load_sem, ready, ready_far, zs, zr, ps, pr, cs, cr, ks, kr, qs, qr, ns, nr, fs, fr,
 ):
     row, col = lax.axis_index("row"), lax.axis_index("col")
     x, y = row // 4, col % 4
@@ -80,11 +79,24 @@
     squeeze[...] = ((r // 12) * 16 + r % 12 == c).astype(BF16)
 
     loads[0].wait()
+    column = pl.multiple_of(core * 384 + lax.rem(x, 3) * 128, 128)
     pad = (iota((16, 12), 0) == iota((16, 12), 1)).astype(BF16)
-    for t in range(3):
-        column = pl.multiple_of(core * 384 + t * 128, 128)
-        own3[t] = dot(pad, density_ref[:, pl.ds(column, 128)]).astype(BF16)
-    tile[Z_OWN] = own3[lax.rem(x, 3)]
+    tile[Z_OWN] = dot(pad, density_ref[:, pl.ds(column, 128)]).astype(BF16)
+
+    pl.semaphore_wait(barrier, len(greet))
+    for d in (-4, 4):
+        pl.semaphore_signal(ready, inc=1, device_id=at_z(d), device_id_type=MESH)
+
+    def z_copy(n):
+        return remote(tile.at[Z_OWN], tile.at[n], zs.at[n], zr.at[n], at_z(n - 4))
+
+    z_up = remote(tile.at[pl.ds(4, 4)], tile.at[pl.ds(8, 4)], zs.at[8], zr.at[8], at_z(4))
+    z_down = remote(tile.at[pl.ds(0, 4)], tile.at[pl.ds(12, 4)], zs.at[9], zr.at[9], at_z(-4))
+
+    @pl.when(x < 3)
+    def _():
+        for n in (0, 1, 7, 2, 6, 3, 5):
+            z_copy(n).start()
 
     for load in loads[1:]:
         load.wait()
@@ -97,26 +109,6 @@
                 keep = (lane < sizes_ref[k] * mask_ref[i, p, k]).astype(F32).astype(BF16)
                 block = raw[p, pl.ds(i * 128, 128), pl.ds(k * 128, 128)]
                 screened[p, pl.ds(i * 128, 128), pl.ds(k * 128, 128)] = block * (present_row * keep)
-
-    pl.semaphore_wait(barrier, len(greet))
-    for d in (-8, 8):
-        pl.semaphore_signal(ready, inc=1, device_id=at_z(d), device_id_type=MESH)
-
-    def z_copy(n):
-        if n < 12:
-            return remote(tile.at[Z_OWN], tile.at[n], zs.at[n], zr.at[n], at_z(Z_SLOTS[n]))
-        return remote(own3, tile3.at[n - 12], zs.at[n], zr.at[n], at_z(Z_SLOTS[n]))
-
-    @pl.when(x < 3)
-    def _():
-        for n in sorted(range(12), key=lambda n: -abs(Z_SLOTS[n])):
-            if n != Z_OWN:
-                z_copy(n).start()
-
-    @pl.when(x == 3)
-    def _():
-        for n in range(12, 16):
-            z_copy(n).start()
 
     @pl.loop(0, 6)
     def _(i):
@@ -143,66 +135,52 @@
                     left[p, pl.ds(to, 48)] = moved[at : at + 48]
             right[p, rows] = dot(spread[rows], screened[p]).astype(BF16)
 
-    prepare(0)
-
-    def block(g, sx, sy):
-        at = pl.multiple_of(g * 384 + sy * 96, 16)
-        return dens.at[core, sx, pl.ds(at, 96 if g == 0 else 48)]
-
-    def block3(sy):
-        return dens.at[core, :, pl.ds(pl.multiple_of(384 + sy * 96 + 48, 16), 48)]
-
     def plane_copy(g, n):
-        mine = block(g, x, y)
-        return remote(mine, mine, ps.at[g, n], pr.at[g * 12 + x * 4 + y], in_plane(*PLANE[n]))
-
-    def plane_copy3(n):
-        mine = block3(y)
-        return remote(mine, mine, ps.at[1, n], pr.at[24 + y], in_plane(*PLANE[n]))
+        mine = dens.at[core, x, pl.ds(pl.multiple_of(g * 384 + y * 96, 16), 96)]
+        return remote(
+            mine, mine, ps.at[g, n], pr.at[(g * 3 + x) * 4 + y], in_plane(*PLANE[n])
+        )
+
+    def spread_plane(g):
+        mine = pl.ds(pl.multiple_of(g * 384 + y * 96, 16), 96)
+        rows = tile[g * 8 : g * 8 + 8].reshape(128, 128)
+        dens[core, x, mine] = dot(squeeze[...], rows).astype(BF16)
+        for n in range(len(PLANE)):
+            plane_copy(g, n).start()
 
     @pl.when(x < 3)
     def _():
-        for g in range(2):
-            slots = range(8) if g == 0 else range(8, 12)
-            for n in slots:
-                if n != Z_OWN:
-                    z_copy(n).wait()
-            size = len(slots)
-            rows = tile[slots[0] : slots[0] + size].reshape(size * 16, 128)
-            packed = dot(squeeze[: size * 12, : size * 16], rows).astype(BF16)
-            dens[core, x, pl.ds(pl.multiple_of(g * 384 + y * 96, 16), size * 12)] = packed
-            for n in range(len(PLANE)):
-                plane_copy(g, n).start()
-
-    @pl.when(x == 3)
+        for n in (5, 6, 7):
+            z_copy(n).wait()
+        z_up.start()
+        for n in (3, 2, 1, 0):
+            z_copy(n).wait()
+        z_down.start()
+        spread_plane(0)
+
+    prepare(0)
+
+    @pl.when(x < 3)
     def _():
-        for n in range(12, 16):
-            z_copy(n).wait()
-        for t in range(3):
-            packed = dot(squeeze[:48, :64], tile3[:, t].reshape(64, 128)).astype(BF16)
-            dens[core, t, pl.ds(pl.multiple_of(384 + y * 96 + 48, 16), 48)] = packed
-        for n in range(len(PLANE)):
-            plane_copy3(n).start()
+        z_up.wait()
+        z_down.wait()
+        spread_plane(1)
 
     prepare(1)
+    pl.semaphore_wait(ready, 2)
+    for d in (-8, 8):
+        pl.semaphore_signal(ready_far, inc=1, device_id=at_z(d), device_id_type=MESH)
 
     c_copies = []
     for g in range(2):
-        if g == 1:
-            for sy in range(4):
-
-                @pl.when(jnp.logical_or(x != 3, y != sy))
-                def _():
-                    remote(block3(sy), block3(sy), ps.at[0, 0], pr.at[24 + sy], sibling).wait_recv()
-
         for sx in range(3):
             for sy in range(4):
+                block = dens.at[core, sx, pl.ds(g * 384 + sy * 96, 96)]
 
                 @pl.when(jnp.logical_or(x != sx, y != sy))
                 def _():
-                    arrived = block(g, sx, sy)
                     remote(
-                        arrived, arrived, ps.at[0, 0], pr.at[g * 12 + sx * 4 + sy], sibling
+                        block, block, ps.at[0, 0], pr.at[(g * 3 + sx) * 4 + sy], sibling
                     ).wait_recv()
 
             whole = dens.at[core, sx, pl.ds(g * 384, 384)]
@@ -325,7 +303,7 @@
         second = jnp.concatenate([total[b * 12 + 8 : b * 12 + 12]] * 2, axis=0)
         f_send[b] = jnp.where(lanes < 48, first, pltpu.roll(second, 48, 1))
         f_send[4 + b] = jnp.where(lanes < 48, pltpu.roll(first, 80, 1), second)
-    pl.semaphore_wait(ready, 2)
+    pl.semaphore_wait(ready_far, 2)
     f_copies = []
     for n, d in enumerate(Z_FAR):
         target = wrap(z + d, 32) // 4
@@ -345,11 +323,6 @@
         for g in range(2):
             for n in range(len(PLANE)):
                 plane_copy(g, n).wait_send()
-
-    @pl.when(x == 3)
-    def _():
-        for n in range(len(PLANE)):
-            plane_copy3(n).wait_send()
 
     for copy in c_copies + k_copies + q_copies + n_copies + f_copies:
         copy.wait_send()
@@ -374,9 +347,7 @@
             vmem(768, 768),
             vmem(768, 768),
             vmem(96, 128),
-            vmem(12, 16, 128),
-            vmem(3, 16, 128),
-            vmem(4, 3, 16, 128),
+            vmem(16, 16, 128),
             vmem(2, 3, 768, 128),
             vmem(2, 2, 768, 384),
             vmem(3, 384, 256),
@@ -389,8 +360,9 @@
             pltpu.VMEM((7, 8, 128), F32),
             dma(4),
             pltpu.SemaphoreType.REGULAR,
-            dma(16), dma(16),
-            dma(2, 15), dma(28),
+            pltpu.SemaphoreType.REGULAR,
+            dma(10), dma(10),
+            dma(2, 15), dma(24),
             dma(6), dma(6),
             dma(3), dma(3),
             dma(2, 16), dma(2, 16),

time: 75.3 us -> 72.3 us (0.960)
  Pallas kernels: 74.5 us -> 71.5 us
    pallas_call x1, Pallas kernels: 74.5 us -> 71.5 us  [shards(): pl.pallas_call(kernel, out_shape=pltpu.VMEM((12, 48), F32), in_specs=[pl....]
where the time goes in v3:
time: 72.3 us; the launch traced here: 72.1 us
  Pallas kernels  71.5 us (99%)
    pallas_call x1, Pallas kernels, shards(): pl.pallas_call(kernel, out_shape=pltpu.VMEM((12, 48), F32), in_specs=[pl....  71.5 us

profile of v3, /device:TPU:24, one launch (start us, length us, event | category | flops | bytes accessed | tf_op | source)
XLA Modules:
  0.0 72.1 jit_solution(15893170486361154220)
XLA Ops:
  0.0 71.5 %exchange.1 = f32[12,48]{1,0:T(8,128)S(1)} custom-call(s32[6,2,6]{2,1,0:T(2,128)} %bitcast.3, s32[6]{0:T(128)} %sizes_hbm.1, bf16[2,768,768]{2,1,0:T(8,128)(2,1)} %integrals_ref.1, bf16[12,768]{1,0:T(8,128)(2,1)} %density_hbm.1), custom_call_target="tpu_custom_call" | custom-call | tf_op jit(solution)/shard_map/exchange/pallas_call | solution.py:334
  71.5 0.6 copy.6

commit v4 on v3

--- a/solution.py
+++ b/solution.py
@@ -39,7 +39,7 @@
 def kernel(
     mask_hbm, sizes_hbm, integrals_ref, density_hbm, out_ref,
     mask_ref, sizes_ref, density_ref,
-    raw, screened, left, right, swap, spread, squeeze, tile, dens, contracted,
+    raw, screened, left, right, swap, spread, squeeze, tile, dens, partial, contracted,
     k_send, k_land, p_send, p_land, by_column, n_land, f_send, f_land,
     load_sem, ready, ready_far, zs, zr, ps, pr, cs, cr, ks, kr, qs, qr, ns, nr, fs, fr,
 ):
@@ -171,8 +171,11 @@
     for d in (-8, 8):
         pl.semaphore_signal(ready_far, inc=1, device_id=at_z(d), device_id_type=MESH)
 
-    c_copies = []
-    for g in range(2):
+    def pass_on(g, sx, to):
+        whole = dens.at[to, sx, pl.ds(g * 384, 384)]
+        return remote(whole, whole, cs.at[g * 3 + sx], cr.at[g * 3 + sx], sibling)
+
+    def pass_group(g):
         for sx in range(3):
             for sy in range(4):
                 block = dens.at[core, sx, pl.ds(g * 384 + sy * 96, 96)]
@@ -183,26 +186,34 @@
                         block, block, ps.at[0, 0], pr.at[(g * 3 + sx) * 4 + sy], sibling
                     ).wait_recv()
 
-            whole = dens.at[core, sx, pl.ds(g * 384, 384)]
-            c_copies.append(remote(whole, whole, cs.at[g * 3 + sx], cr.at[g * 3 + sx], sibling))
-            c_copies[-1].start()
-
-    def contract(half):
-        density = jnp.concatenate([dens[half, t] for t in range(3)], axis=1)
-
-        @pl.loop(0, 4)
-        def _(i):
-            p, rows = i // 2, pl.ds(pl.multiple_of(i % 2 * 384, 384), 384)
-            contracted[p, half, rows] = dot(left[p, rows], density).astype(BF16)
-
-    contract(core)
-    for g in range(2):
+            pass_on(g, sx, core).start()
+
+    def await_group(g):
         for sx in range(3):
-            whole = dens.at[1 - core, sx, pl.ds(g * 384, 384)]
-            remote(
-                whole, whole, cs.at[g * 3 + sx], cr.at[g * 3 + sx], sibling
-            ).wait_recv()
-    contract(1 - core)
+            pass_on(g, sx, 1 - core).wait_recv()
+
+    def contract(half, g, rows_of):
+        @pl.loop(0, 2)
+        def _(p):
+            rows, depth = pl.ds(rows_of * 384, 384), pl.ds(g * 384, 384)
+            density = jnp.concatenate([dens[half, t, depth] for t in range(3)], axis=1)
+            term = dot(left[p, rows, depth], density)
+            if g == 0:
+                partial[p, half, rows] = term
+            else:
+                contracted[p, half, rows] = (partial[p, half, rows] + term).astype(BF16)
+
+    pass_group(0)
+    contract(core, 0, 0)
+    contract(core, 0, 1)
+    await_group(0)
+    contract(1 - core, 0, 0)
+    contract(1 - core, 0, 1)
+    pass_group(1)
+    contract(core, 1, 0)
+    contract(core, 1, 1)
+    await_group(1)
+    contract(1 - core, 1, 0)
 
     def exchange(half, chunk):
         total = None
@@ -252,10 +263,11 @@
                 ).start()
 
     send_half(0)
-    send_half(1)
+    contract(1 - core, 1, 1)
     own_half(0)
     send_plane(0, 0)
     send_plane(0, 1)
+    send_half(1)
     send_half(2)
     own_half(1)
     send_plane(0, 2)
@@ -324,7 +336,9 @@
             for n in range(len(PLANE)):
                 plane_copy(g, n).wait_send()
 
-    for copy in c_copies + k_copies + q_copies + n_copies + f_copies:
+    for n in range(6):
+        pass_on(n // 3, n % 3, core).wait_send()
+    for copy in k_copies + q_copies + n_copies + f_copies:
         copy.wait_send()
 
 
@@ -349,6 +363,7 @@
             vmem(96, 128),
             vmem(16, 16, 128),
             vmem(2, 3, 768, 128),
+            pltpu.VMEM((2, 2, 768, 384), F32),
             vmem(2, 2, 768, 384),
             vmem(3, 384, 256),
             vmem(3, 384, 256),

time: 72.3 us -> 71.2 us (0.985)
  Pallas kernels: 71.5 us -> 70.3 us
    pallas_call x1, Pallas kernels: 71.5 us -> 70.3 us  [shards(): pl.pallas_call(kernel, out_shape=pltpu.VMEM((12, 48), F32), in_specs=[pl....]
where the time goes in v4:
time: 71.2 us; the launch traced here: 70.9 us
  Pallas kernels  70.3 us (99%)
    pallas_call x1, Pallas kernels, shards(): pl.pallas_call(kernel, out_shape=pltpu.VMEM((12, 48), F32), in_specs=[pl....  70.3 us

profile of v4, /device:TPU:24, one launch (start us, length us, event | category | flops | bytes accessed | tf_op | source)
XLA Modules:
  0.0 70.9 jit_solution(16575728553547543264)
XLA Ops:
  0.0 70.3 %exchange.1 = f32[12,48]{1,0:T(8,128)S(1)} custom-call(s32[6,2,6]{2,1,0:T(2,128)} %bitcast.3, s32[6]{0:T(128)} %sizes_hbm.1, bf16[2,768,768]{2,1,0:T(8,128)(2,1)} %integrals_ref.1, bf16[12,768]{1,0:T(8,128)(2,1)} %density_hbm.1), custom_call_target="tpu_custom_call" | custom-call | tf_op jit(solution)/shard_map/exchange/pallas_call | solution.py:348
  70.3 0.6 copy.6

commit v5 on v4

--- a/solution.py
+++ b/solution.py
@@ -10,9 +10,10 @@
 BF16 = jnp.bfloat16
 
 Z_OWN = 4
-PLANE = [(dx, dy) for dx in range(4) for dy in range(4) if (dx, dy) != (0, 0)]
+FARTHEST = (2, 1, 3, 0)
+PLANE = [(dx, dy) for dx in FARTHEST for dy in FARTHEST if (dx, dy) != (0, 0)]
 Z_NEAR = [-2, -1, 1]
-Z_FAR = [-12, -8, -4, 4, 8, 12, 16]
+Z_FAR = [16, 12, -12, 8, -8, 4, -4]
 Z_GREET = [-4, 4, -3, 3, -2, 2, -1, 1]
 
 
@@ -117,7 +118,7 @@
         origin = (z_lo + 36 - c // 384 * 8 - c % 96 // 12) % 16
         swap[pl.ds(start, 128)] = (origin * 48 + c % 384 // 96 * 12 + c % 12 == r).astype(BF16)
         tail = r - 512
-        part = jnp.where(r < 512, r // 128, tail // 64)
+        part = (y + 6 - jnp.where(r < 512, r // 128, tail // 64)) % 4
         q = jnp.where(r < 512, r % 128, tail % 64 + 128)
         source = q % 48 // 12 * 192 + q // 48 * 48 + part * 12 + q % 12
         spread[pl.ds(start, 128)] = (source == c).astype(BF16)
@@ -251,15 +252,14 @@
 
     parts = [pl.ds(0, 96), pl.ds(96, 48)]
 
-    def send_plane(part, ty):
-        for tx in range(4):
-
-            @pl.when(jnp.logical_or(tx != x, ty != y))
-            def _():
-                slot = (tx - x + 4) % 4 * 4 + (ty - y + 4) % 4
+    def send_plane(part, k):
+        dy = (6 - k) % 4
+        for dx in FARTHEST:
+            if (dx, dy) != (0, 0):
+                slot = dx * 4 + dy
                 remote(
-                    p_send.at[tx * 4 + ty, parts[part]], p_land.at[slot, parts[part]],
-                    qs.at[part, slot], qr.at[part, slot], device(tx, ty, z, core),
+                    p_send.at[(x + dx) % 4 * 4 + k, parts[part]], p_land.at[slot, parts[part]],
+                    qs.at[part, slot], qr.at[part, slot], in_plane(dx, dy),
                 ).start()
 
     send_half(0)
@@ -273,8 +273,8 @@
     send_plane(0, 2)
     send_plane(0, 3)
     own_half(2)
-    for ty in range(4):
-        send_plane(1, ty)
+    for k in range(4):
+        send_plane(1, k)
 
     q_copies = [
         remote(
@@ -285,7 +285,7 @@
     ]
     sums = []
     for part, rows in enumerate(parts):
-        total = p_send[x * 4 + y, rows].astype(F32)
+        total = p_send[x * 4 + 2, rows].astype(F32)
         for slot in range(1, 16):
             q_copies[part * 15 + slot - 1].wait_recv()
             total = total + p_land[slot, rows].astype(F32)

time: 71.2 us -> 69.7 us (0.979)
  Pallas kernels: 70.3 us -> 68.3 us
    pallas_call x1, Pallas kernels: 70.3 us -> 68.3 us  [shards(): pl.pallas_call(kernel, out_shape=pltpu.VMEM((12, 48), F32), in_specs=[pl....]
where the time goes in v5:
time: 69.7 us; the launch traced here: 68.9 us
  Pallas kernels  68.3 us (98%)
    pallas_call x1, Pallas kernels, shards(): pl.pallas_call(kernel, out_shape=pltpu.VMEM((12, 48), F32), in_specs=[pl....  68.3 us

profile of v5, /device:TPU:24, one launch (start us, length us, event | category | flops | bytes accessed | tf_op | source)
XLA Modules:
  0.0 68.9 jit_solution(8516557985729342388)
XLA Ops:
  0.0 68.3 %exchange.1 = f32[12,48]{1,0:T(8,128)S(1)} custom-call(s32[6,2,6]{2,1,0:T(2,128)} %bitcast.3, s32[6]{0:T(128)} %sizes_hbm.1, bf16[2,768,768]{2,1,0:T(8,128)(2,1)} %integrals_ref.1, bf16[12,768]{1,0:T(8,128)(2,1)} %density_hbm.1), custom_call_target="tpu_custom_call" | custom-call | tf_op jit(solution)/shard_map/exchange/pallas_call | solution.py:348
  68.3 0.6 copy.6
